TPU v7x, 256 devices: a whole 4x4x8 slice. The times are simulated.
256 devices in a mesh: row: 8 (over x, core), col: 32 (over z, y).
Axes of the slice: x: 4, y: 4, z: 8, core: 2. Of those that a mesh axis runs over, the one named last changes fastest.
Arguments:
- tensor: float32 [2048, 2048, 128], P('row', 'col'), may hold values from -140 to 140
- factor_b0: float32 [2048, 32], P('col'), may hold values from -4 to 4
- factor_c0: float32 [128, 32], replicated, may hold values from -4 to 4
Outputs:
- factor_a: float32 [2048, 32], P('row')
- factor_b: float32 [2048, 32], P('col')
- factor_c: float32 [128, 32], replicated
- weights: float32 [32], replicated
All inputs are finite; a program needn't handle non-finite values.
Results may differ from a plain program's by a relative error of at most 0.00013.
Values sent between devices are 32-bit elements; how exact they have to be, the bound alone decides.
A program may use at most 64 MiB of HBM per device.

v0:
```python
import jax
import jax.numpy as jnp
from jax import lax
from jax.sharding import PartitionSpec as P

SWEEPS = 2


EPSILON = 1e-06


def cross_gram(left, right):
    return jnp.dot(
        left.T, right, precision=lax.Precision.HIGHEST, preferred_element_type=jnp.float32
    )


def solve_rows(mttkrp, system):
    cholesky_low = jnp.linalg.cholesky(system)
    return jax.scipy.linalg.cho_solve((cholesky_low, True), mttkrp.T).T


def scaled(moments, count):
    scales = jnp.sqrt(jnp.diagonal(moments) / count + EPSILON)
    return (scales, moments / (scales[:, None] * scales[None, :]))


def solve_third(part_c, system_c):
    summed_c = lax.psum(part_c, ("row", "col"))
    return solve_rows(summed_c, system_c)


def shards(tensor, factor_b0, factor_c0):
    block_i, block_j, third_len = tensor.shape
    rank = factor_b0.shape[1]
    total_i = block_i * lax.axis_size("row")
    total_j = block_j * lax.axis_size("col")
    gram_b = lax.psum(cross_gram(factor_b0, factor_b0), "col")
    gram_c = cross_gram(factor_c0, factor_c0)

    def one_sweep(sweep_index, carry):
        a_block, b_block, c_all, gram_b, gram_c, weights = carry
        y_rows = jnp.einsum("ijk,jr->irk", tensor, b_block, precision=lax.Precision.HIGHEST)
        part_a = jnp.sum(y_rows * c_all.T[None, :, :], axis=2)
        system_a = gram_b * gram_c
        owned_rows = lax.psum_scatter(part_a, "col", scatter_dimension=0, tiled=True)
        solved = solve_rows(owned_rows, system_a)
        moments = lax.psum(cross_gram(solved, solved), ("row", "col"))
        scales, gram_a = scaled(moments, total_i)
        a_block = lax.all_gather(solved / scales[None, :], "col", axis=0, tiled=True)
        crossed = jnp.einsum("ijk,ir->jrk", tensor, a_block, precision=lax.Precision.HIGHEST)
        part_b = jnp.sum(crossed * c_all.T[None, :, :], axis=2)
        owned_b = lax.psum_scatter(part_b, "row", scatter_dimension=0, tiled=True)
        solved_b = solve_rows(owned_b, gram_a * gram_c)
        moments_b = lax.psum(cross_gram(solved_b, solved_b), ("row", "col"))
        scales_b, gram_b = scaled(moments_b, total_j)
        b_block = lax.all_gather(solved_b / scales_b[None, :], "row", axis=0, tiled=True)
        part_c = jnp.einsum("jrk,jr->kr", crossed, b_block, precision=lax.Precision.HIGHEST)
        solved_c = solve_third(part_c, gram_a * gram_b)
        weights = jnp.sqrt(jnp.sum(solved_c * solved_c, axis=0) / third_len + EPSILON)
        c_all = solved_c / weights[None, :]
        gram_c = cross_gram(c_all, c_all)
        return (a_block, b_block, c_all, gram_b, gram_c, weights)

    start = (
        jnp.zeros((block_i, rank), jnp.float32),
        factor_b0,
        factor_c0,
        gram_b,
        gram_c,
        jnp.zeros((rank,), jnp.float32),
    )
    a_block, b_block, c_all, gram_b, gram_c, weights = lax.fori_loop(0, SWEEPS, one_sweep, start)
    return (a_block, b_block, c_all, weights)


def solution(mesh):
    return jax.shard_map(
        shards,
        mesh=mesh,
        in_specs=(P("row", "col", None), P("col", None), P()),
        out_specs=(P("row", None), P("col", None), P(), P()),
        check_vma=False,
    )
```

profile of v0, /device:TPU:1, one launch (start us, length us, event | category | flops | bytes accessed | tf_op | source)
XLA Modules:
  0.0 1137.1 jit_solution(733284977786943742)
XLA Ops:
  0.6 0.7 copy.114
  1.5 0.9 fusion.33
  2.4 118.9 %psum.28 = f32[32,32]{1,0:T(8,128)S(1)} all-reduce(f32[32,32]{1,0:T(8,128)S(1)} %fusion.33), channel_id=1, replica_groups=mesh['row'=8,'col'=32] {'col'}, use_global_device_ids=true, to_apply=%region_0.0 | all-reduce | flops 1024 | bytes 8192 | tf_op jit(solution)/shard_map/psum | solution.py:38
  121.4 0.8 copy.55
  122.3 11.5 %copy.57 = f32[256,64,128]{2,0,1:T(8,128)} copy(f32[256,64,128]{2,1,0:T(8,128)} %param.8) | data formatting | bytes 16777216 | tf_op jit(solution)/shard_map/while | solution.py:73
  133.7 1001.1 %while.20 = (s32[]{:T(128)}, f32[256,32]{1,0:T(8,128)}, f32[64,32]{1,0:T(8,128)S(1)}, f32[128,32]{0,1:T(8,128)S(1)}, f32[32,32]{0,1:T(8,128)S(1)}, /*index=5*/f3...) while((s32[]{:T(128)}, f32[256,32]{1,0:T(8,128)}, ...), condition=%wide.region_12.15_spmd, body=%wide.region_1.0_spmd.sunk | while | flops 1621744384 | bytes 19761416 | solution.py:73
  133.7 0.6 dynamic-slice.14
  135.0 0.6 dynamic-slice.15
  136.4 2.9 cholesky.200
  139.3 0.6 compare_reduce_fusion.6
  140.0 0.7 fusion.109
  140.6 2.4 custom-call.30
  143.1 13.2 %multiply_reduce_fusion.6 = f32[32,256]{0,1:T(8,128)S(1)} fusion(f32[256,64,128]{2,0,1:T(8,128)} %get-tuple-element.213, f32[32,128]{1,0:T(8,128)S(1)} %bitcast.159, f32[64,32]{1,0:T(8,128)S(1)} %get-tuple-element.195), kind=kOutput, calls=%fused_computation.4.clone.1 | convolution fusion | flops 807395328 | bytes 8445952 | tf_op jit(solution)/shard_map/while/body/eval_jaxpr/ijk,jr->irk/dot_general | solution.py:43
  156.4 110.4 %all-reduce.4 = f32[256,32]{0,1:T(8,128)S(1)} all-reduce(f32[256,32]{0,1:T(8,128)S(1)} %copy.85), channel_id=2, replica_groups=mesh['row'=8,'col'=32] {'col'}, use_global_device_ids=true, to_apply=%region_5.6.clone | all-reduce | flops 8192 | bytes 65536 | tf_op jit(solution)/shard_map/while
  266.8 0.3 fusion.110
  267.4 128.9 %psum.32 = f32[32,32]{0,1:T(8,128)S(1)} all-reduce(f32[32,32]{0,1:T(8,128)S(1)} %fusion.112), channel_id=1, replica_groups=mesh['row'=8,'col'=32] {'row','col'}, use_global_device_ids=true, to_apply=%region_6.8 | all-reduce | flops 1024 | bytes 8192 | tf_op jit(solution)/shard_map/while/body/eval_jaxpr/psum | solution.py:48
  396.4 0.7 gather_fusion
  397.3 2.9 cholesky.201
  400.3 0.6 compare_reduce_fusion.7
  400.9 0.7 fusion.115
  401.6 2.4 custom-call.31
  404.0 32.0 %all_gather.8 = f32[256,32]{1,0:T(8,128)S(1)} all-gather(f32[8,32]{1,0:T(8,128)S(1)} %divide_bitcast_fusion.4), channel_id=1, replica_groups=mesh['row'=8,'col'=32] {'col'}, dimensions={0}, use_global_device_ids=true | all-gather | bytes 33792 | tf_op jit(solution)/shard_map/while/body/eval_jaxpr/all_gather | solution.py:50
  435.9 7.5 multiply_reduce_fusion.7
  443.4 31.2 %all-reduce.5 = f32[64,32]{1,0:T(8,128)S(1)} all-reduce(f32[64,32]{1,0:T(8,128)S(1)} %get-tuple-element.174), channel_id=3, replica_groups=mesh['row'=8,'col'=32] {'row'}, use_global_device_ids=true, to_apply=%region_8.10.clone | all-reduce | flops 2048 | bytes 16384 | tf_op jit(solution)/shard_map/while
  475.1 76.2 %psum.33 = f32[32,32]{0,1:T(8,128)S(1)} all-reduce(f32[32,32]{0,1:T(8,128)S(1)} %fusion.118), channel_id=1, replica_groups=mesh['row'=8,'col'=32] {'row','col'}, use_global_device_ids=true, to_apply=%region_9.11 | all-reduce | flops 1024 | bytes 8192 | tf_op jit(solution)/shard_map/while/body/eval_jaxpr/psum | solution.py:55
  551.3 0.7 gather_fusion.1
  552.2 2.9 cholesky.202
  555.2 0.6 compare_reduce_fusion.8
  555.8 0.7 fusion.122
  556.5 2.4 custom-call.32
  558.9 13.5 %all_gather.9 = f32[64,32]{1,0:T(8,128)S(1)} all-gather(f32[8,32]{1,0:T(8,128)S(1)} %divide_bitcast_fusion.5), channel_id=1, replica_groups=mesh['row'=8,'col'=32] {'row'}, dimensions={0}, use_global_device_ids=true | all-gather | bytes 9216 | tf_op jit(solution)/shard_map/while/body/eval_jaxpr/all_gather | solution.py:57
  572.5 1.5 fusion.119
  574.0 72.8 %psum.34 = f32[128,32]{0,1:T(8,128)S(1)} all-reduce(f32[128,32]{0,1:T(8,128)S(1)} %bitcast.162), channel_id=1, replica_groups=mesh['row'=8,'col'=32] {'row','col'}, use_global_device_ids=true, to_apply=%region_10.12 | all-reduce | flops 4096 | bytes 32768 | tf_op jit(solution)/shard_map/while/body/eval_jaxpr/psum | solution.py:29
  647.5 0.3 copy-done.2
  647.8 0.6 dynamic-slice.14
  649.0 0.6 dynamic-slice.15
  650.4 2.9 cholesky.200
  653.4 0.6 compare_reduce_fusion.6
  654.0 0.7 fusion.109
  654.7 2.4 custom-call.30
  657.1 13.2 %multiply_reduce_fusion.6 = f32[32,256]{0,1:T(8,128)S(1)} fusion(f32[256,64,128]{2,0,1:T(8,128)} %get-tuple-element.213, f32[32,128]{1,0:T(8,128)S(1)} %bitcast.159, f32[64,32]{1,0:T(8,128)S(1)} %get-tuple-element.195), kind=kOutput, calls=%fused_computation.4.clone.1 | convolution fusion | flops 807395328 | bytes 8445952 | tf_op jit(solution)/shard_map/while/body/eval_jaxpr/ijk,jr->irk/dot_general | solution.py:43
  670.4 112.5 %all-reduce.4 = f32[256,32]{0,1:T(8,128)S(1)} all-reduce(f32[256,32]{0,1:T(8,128)S(1)} %copy.85), channel_id=2, replica_groups=mesh['row'=8,'col'=32] {'col'}, use_global_device_ids=true, to_apply=%region_5.6.clone | all-reduce | flops 8192 | bytes 65536 | tf_op jit(solution)/shard_map/while
  782.9 0.3 fusion.110
  783.5 100.4 %psum.32 = f32[32,32]{0,1:T(8,128)S(1)} all-reduce(f32[32,32]{0,1:T(8,128)S(1)} %fusion.112), channel_id=1, replica_groups=mesh['row'=8,'col'=32] {'row','col'}, use_global_device_ids=true, to_apply=%region_6.8 | all-reduce | flops 1024 | bytes 8192 | tf_op jit(solution)/shard_map/while/body/eval_jaxpr/psum | solution.py:48
  883.9 0.7 gather_fusion
  884.8 2.9 cholesky.201
  887.8 0.6 compare_reduce_fusion.7
  888.4 0.7 fusion.115
  889.1 2.4 custom-call.31
  891.5 31.9 %all_gather.8 = f32[256,32]{1,0:T(8,128)S(1)} all-gather(f32[8,32]{1,0:T(8,128)S(1)} %divide_bitcast_fusion.4), channel_id=1, replica_groups=mesh['row'=8,'col'=32] {'col'}, dimensions={0}, use_global_device_ids=true | all-gather | bytes 33792 | tf_op jit(solution)/shard_map/while/body/eval_jaxpr/all_gather | solution.py:50
  923.4 7.5 multiply_reduce_fusion.7
  930.9 30.8 %all-reduce.5 = f32[64,32]{1,0:T(8,128)S(1)} all-reduce(f32[64,32]{1,0:T(8,128)S(1)} %get-tuple-element.174), channel_id=3, replica_groups=mesh['row'=8,'col'=32] {'row'}, use_global_device_ids=true, to_apply=%region_8.10.clone | all-reduce | flops 2048 | bytes 16384 | tf_op jit(solution)/shard_map/while
  962.2 76.0 %psum.33 = f32[32,32]{0,1:T(8,128)S(1)} all-reduce(f32[32,32]{0,1:T(8,128)S(1)} %fusion.118), channel_id=1, replica_groups=mesh['row'=8,'col'=32] {'row','col'}, use_global_device_ids=true, to_apply=%region_9.11 | all-reduce | flops 1024 | bytes 8192 | tf_op jit(solution)/shard_map/while/body/eval_jaxpr/psum | solution.py:55
  1038.2 0.7 gather_fusion.1
  1039.1 2.9 cholesky.202
  1042.0 0.6 compare_reduce_fusion.8
  1042.7 0.7 fusion.122
  1043.4 2.4 custom-call.32
  1045.8 13.3 %all_gather.9 = f32[64,32]{1,0:T(8,128)S(1)} all-gather(f32[8,32]{1,0:T(8,128)S(1)} %divide_bitcast_fusion.5), channel_id=1, replica_groups=mesh['row'=8,'col'=32] {'row'}, dimensions={0}, use_global_device_ids=true | all-gather | bytes 9216 | tf_op jit(solution)/shard_map/while/body/eval_jaxpr/all_gather | solution.py:57
  1059.2 1.5 fusion.119
  1060.6 73.1 %psum.34 = f32[128,32]{0,1:T(8,128)S(1)} all-reduce(f32[128,32]{0,1:T(8,128)S(1)} %bitcast.162), channel_id=1, replica_groups=mesh['row'=8,'col'=32] {'row','col'}, use_global_device_ids=true, to_apply=%region_10.12 | all-reduce | flops 4096 | bytes 32768 | tf_op jit(solution)/shard_map/while/body/eval_jaxpr/psum | solution.py:29
  1134.5 0.3 copy-done.2
  1134.8 0.7 copy.59
  1135.5 1.6 copy.58
  (76 shorter events, 4.9 us)
Async XLA Ops:
  122.2 11.5 %copy-start.3 = (u32[256]{0:T(256)S(1)}, u32[256]{0:T(256)}, u32[]{:S(2)}) copy-start(u32[256]{0:T(256)} %constant.139) | copy-start | bytes 3076
  122.3 11.5 %copy-start.4 = (u32[256]{0:T(256)S(1)}, u32[256]{0:T(256)}, u32[]{:S(2)}) copy-start(u32[256]{0:T(256)} %constant.136) | copy-start | bytes 3076
  435.9 211.6 %copy-start.1 = (f32[256,32]{1,0:T(8,128)}, f32[256,32]{1,0:T(8,128)S(1)}, u32[]{:S(2)}) copy-start(f32[256,32]{1,0:T(8,128)S(1)} %all_gather.8) | copy-start | bytes 98308 | tf_op jit(solution)/shard_map/while
  647.3 0.5 copy-start.2
  923.4 211.1 %copy-start.1 = (f32[256,32]{1,0:T(8,128)}, f32[256,32]{1,0:T(8,128)S(1)}, u32[]{:S(2)}) copy-start(f32[256,32]{1,0:T(8,128)S(1)} %all_gather.8) | copy-start | bytes 98308 | tf_op jit(solution)/shard_map/while
  1134.3 0.5 copy-start.2
  1134.8 2.3 copy-start
where the time goes:
time: 1140 us
  blocking collectives  1020 us (89%)
  matrix products  48.9 us (4%)
  other arithmetic  40.7 us (4%)
  local copies, waits for them, and re-layouts  21.9 us (2%)
    while x4, blocking collectives  285 us
    psum x2, blocking collectives, one_sweep(): moments = lax.psum(cross_gram(solved, solved), ('row', 'col'))  229 us
    psum x2, blocking collectives, one_sweep(): moments_b = lax.psum(cross_gram(solved_b, solved_b), ('row', 'col'))  152 us
    psum x2, blocking collectives, solve_third(): summed_c = lax.psum(part_c, ('row', 'col'))  146 us
    psum x1, blocking collectives, shards(): gram_b = lax.psum(cross_gram(factor_b0, factor_b0), 'col')  119 us
    all_gather x2, blocking collectives, one_sweep(): lax.all_gather(solved / scales[None, :], 'col', axis=0, tiled=True)  63.9 us
    all_gather x2, blocking collectives, one_sweep(): lax.all_gather(solved_b / scales_b[None, :], 'row', axis=0, tiled=True)  26.8 us
    dot_general x2, matrix products, one_sweep(): jnp.einsum('ijk,jr->irk', tensor, b_block, precision=lax.Precision.HIGHEST)  26.5 us

commit v1 on v0

v1 whole, which is shorter than its diff:
```python
import functools

import jax
import jax.numpy as jnp
from jax import lax
from jax.experimental import pallas as pl
from jax.experimental.pallas import tpu as pltpu
from jax.sharding import PartitionSpec as P

SWEEPS = 2
EPSILON = 1e-06
F32 = jnp.float32
BF16 = jnp.bfloat16
MESH = pl.DeviceIdType.MESH
NT = (((1,), (1,)), ((), ()))
NN = (((1,), (0,)), ((), ()))
TN = (((0,), (0,)), ((), ()))


def exact(left, right, dims):
    return lax.dot_general(
        left, right, dims, precision=lax.Precision.HIGHEST, preferred_element_type=F32
    )


def fast(left, right, dims):
    return lax.dot_general(left, right, dims, preferred_element_type=F32)


def split(x):
    high = x.astype(BF16)
    return high, (x - high.astype(F32)).astype(BF16)


def pack_square(g):
    return jnp.concatenate([g[8 * q : 8 * q + 8, :] for q in range(4)], axis=1)


def unpack_square(p):
    return jnp.concatenate([p[:, 32 * q : 32 * q + 32] for q in range(4)], axis=0)


def inverse(system):
    row = lax.broadcasted_iota(jnp.int32, (32, 32), 0)
    lane = lax.broadcasted_iota(jnp.int32, (32, 32), 1)
    unit = jnp.where(row == lane, 1.0, 0.0).astype(F32)
    both = jnp.concatenate([system, unit], axis=1)
    parts = [both[8 * q : 8 * q + 8] for q in range(4)]
    sub = lax.broadcasted_iota(jnp.int32, (8, 64), 0)
    out = []
    for k in range(32):
        q, s = divmod(k, 8)
        pivot_row = jnp.broadcast_to(parts[q][s : s + 1, :], (8, 64))
        pivot = jnp.broadcast_to(pivot_row[:, k : k + 1], (8, 64))
        scaled_row = pivot_row * (1.0 / pivot)
        out.append((pivot_row * lax.rsqrt(pivot))[0:1, 32:])
        for t in range(q, 4):
            low = jnp.broadcast_to(parts[t][:, k : k + 1], (8, 64))
            if t == q:
                low = jnp.where(sub > s, low, 0.0)
            parts[t] = parts[t] - low * scaled_row
    w = jnp.concatenate(out, axis=0)
    return exact(w, w, TN)


def scales_of(moments, count):
    row = lax.broadcasted_iota(jnp.int32, (32, 32), 0)
    lane = lax.broadcasted_iota(jnp.int32, (32, 32), 1)
    diagonal = jnp.where(row == lane, moments, 0.0)
    down = jnp.sqrt(jnp.sum(diagonal, axis=1, keepdims=True) / count + EPSILON)
    across = jnp.sqrt(jnp.sum(diagonal, axis=0, keepdims=True) / count + EPSILON)
    return down, moments / (down * across)


def kernel(
    total_i, total_j,
    tensor, b_in, c_in,
    a_out, b_out, c_out, w_out,
    staged, high, low, wide_b, kr, y,
    gram_src, gram_got, ma_src, ma_got, ma_sum, ma_all,
    mom_src, mom_got, mb_src, mb_got,
    mc_src, mc_got, mc_mid, mc_col, mc_sum, mc_all,
    load_sem, gram_sem, ma_sem, maz_sem, mom_sem, mb_sem, mc_sem, mcc_sem, mcr_sem,
):
    row, col = lax.axis_index("row"), lax.axis_index("col")
    z, y_at = col // 4, lax.rem(col, 4)

    barrier = pltpu.get_barrier_semaphore()

    def greet_col(step, carry):
        pl.semaphore_signal(
            barrier, inc=1, device_id=(row, lax.rem(col + step, 32)), device_id_type=MESH
        )
        return carry

    def greet_row(step, carry):
        pl.semaphore_signal(
            barrier, inc=1, device_id=(lax.rem(row + step, 8), col), device_id_type=MESH
        )
        return carry

    lax.fori_loop(1, 32, greet_col, 0)
    lax.fori_loop(1, 8, greet_row, 0)

    def load(j, carry):
        pltpu.make_async_copy(tensor.at[:, j, :], staged.at[j], load_sem.at[j // 8]).start()
        return carry

    lax.fori_loop(0, 64, load, 0)

    sent = []

    def finish(got, count, sem):
        view = got.at[pl.ds(0, count)]
        pltpu.make_async_copy(view, view, sem).wait()

    def to_col(source, got, sems):
        def one(step, carry):
            there = lax.rem(col + step, 32)
            pltpu.make_async_remote_copy(
                src_ref=source, dst_ref=got.at[col], send_sem=sems.at[0], recv_sem=sems.at[1],
                device_id=(row, there), device_id_type=MESH,
            ).start()
            return carry

        lax.fori_loop(1, 32, one, 0)
        sent.append((got, 31, sems.at[0]))

    def to_row(pick, got, sems):
        def one(step, carry):
            there = lax.rem(row + step, 8)
            pltpu.make_async_remote_copy(
                src_ref=pick(there), dst_ref=got.at[row], send_sem=sems.at[0],
                recv_sem=sems.at[1], device_id=(there, col), device_id_type=MESH,
            ).start()
            return carry

        lax.fori_loop(1, 8, one, 0)
        sent.append((got, 7, sems.at[0]))

    def total(got, count):
        acc = got[0]
        for at in range(1, count):
            acc = acc + got[at]
        return acc

    bt = b_in[...]
    ct = c_in[...]
    gram_c = exact(ct, ct, NT)
    gram_src[0] = pack_square(exact(bt, bt, NT))

    def widen(values):
        for j in range(64):
            wide_b[j] = jnp.broadcast_to(values[:, j : j + 1], (32, 128))

    def khatri_rao(third):
        def body(pair, carry):
            h, l = split(
                jnp.concatenate([wide_b[2 * pair] * third, wide_b[2 * pair + 1] * third], axis=1)
            )
            kr[pair, 0:32, :] = h
            kr[pair, 32:64, :] = l
            return carry

        lax.fori_loop(0, 32, body, 0)

    widen(bt)
    khatri_rao(ct)

    pl.semaphore_wait(barrier, 38)
    to_col(gram_src.at[0], gram_got.at[0], gram_sem.at[0])
    gram_got[0, col] = gram_src[0]

    def unpack(group, carry):
        view = staged.at[pl.ds(8 * group, 8)]
        pltpu.make_async_copy(view, view, load_sem.at[group]).wait()
        for at in range(4):
            pair = 4 * group + at
            h, l = split(jnp.concatenate([staged[2 * pair], staged[2 * pair + 1]], axis=1))
            high[pair] = h
            low[pair] = l
        return carry

    lax.fori_loop(0, 8, unpack, 0)

    gram_a = None
    for sweep in range(SWEEPS):
        def product_a(pair, acc):
            p = fast(kr[pair], high[pair], NT)
            q = fast(kr[pair, 0:32, :], low[pair], NT)
            return acc + (p[:32] + p[32:] + q)

        part = lax.fori_loop(0, 32, product_a, jnp.zeros((32, 256), F32), unroll=4)
        for tile in range(8):
            q, half = divmod(tile, 2)
            ma_src[sweep, tile] = part[8 * q : 8 * q + 8, 128 * half : 128 * half + 128]

        def send_tile(step, carry):
            there = lax.rem(col + step, 32)
            pltpu.make_async_remote_copy(
                src_ref=ma_src.at[sweep, there // 4], dst_ref=ma_got.at[sweep, col],
                send_sem=ma_sem.at[sweep, 0], recv_sem=ma_sem.at[sweep, 1],
                device_id=(row, there), device_id_type=MESH,
            ).start()
            return carry

        lax.fori_loop(1, 32, send_tile, 0)
        sent.append((ma_got.at[sweep], 31, ma_sem.at[sweep, 0]))
        ma_got[sweep, col] = ma_src[sweep, z]

        if sweep == 0:
            finish(gram_got.at[0], 31, gram_sem.at[0, 1])
            gram_b = unpack_square(total(gram_got.at[0], 32))
        inverse_a = inverse(gram_b * gram_c)

        finish(ma_got.at[sweep], 31, ma_sem.at[sweep, 1])
        summed = total(ma_got.at[sweep], 32)
        ma_sum[sweep] = summed

        def send_sum(step, carry):
            there = lax.rem(z + step, 8)
            pltpu.make_async_remote_copy(
                src_ref=ma_sum.at[sweep], dst_ref=ma_all.at[sweep, z],
                send_sem=maz_sem.at[sweep, 0], recv_sem=maz_sem.at[sweep, 1],
                device_id=(row, there * 4 + y_at), device_id_type=MESH,
            ).start()
            return carry

        lax.fori_loop(1, 8, send_sum, 0)
        sent.append((ma_all.at[sweep], 7, maz_sem.at[sweep, 0]))
        ma_all[sweep, z] = summed
        finish(ma_all.at[sweep], 7, maz_sem.at[sweep, 1])
        m_a = jnp.concatenate(
            [
                jnp.concatenate([ma_all[sweep, 2 * q], ma_all[sweep, 2 * q + 1]], axis=1)
                for q in range(4)
            ],
            axis=0,
        )
        solved_a = exact(inverse_a, m_a, NN)

        mom_src[sweep] = pack_square(exact(solved_a, solved_a, NT))
        to_row(lambda there: mom_src.at[sweep], mom_got.at[sweep], mom_sem.at[sweep])
        mom_got[sweep, row] = mom_src[sweep]
        a_high, a_low = split(solved_a)
        a_both = jnp.concatenate([a_high, a_low], axis=0)

        def product_y(pair, carry):
            p = fast(a_both, high[pair], NN)
            q = fast(a_high, low[pair], NN)
            y[pair] = p[:32] + p[32:] + q
            return carry

        lax.fori_loop(0, 32, product_y, 0, unroll=4)
        lane = lax.broadcasted_iota(jnp.int32, (32, 64), 1)

        def reduce_y(pair, acc):
            r = y[pair]
            first = jnp.sum(r[:, :128] * ct, axis=1, keepdims=True)
            second = jnp.sum(r[:, 128:] * ct, axis=1, keepdims=True)
            return jnp.where(lane == 2 * pair, first, jnp.where(lane == 2 * pair + 1, second, acc))

        part = lax.fori_loop(0, 32, reduce_y, jnp.zeros((32, 64), F32), unroll=4)
        mb_src[sweep] = jnp.concatenate([part[:16], part[16:]], axis=1)
        to_row(lambda there: mb_src.at[sweep], mb_got.at[sweep], mb_sem.at[sweep])
        mb_got[sweep, row] = mb_src[sweep]

        finish(mom_got.at[sweep], 7, mom_sem.at[sweep, 1])
        scale_a, gram_a = scales_of(unpack_square(total(mom_got.at[sweep], 8)), total_i)
        inverse_b = inverse(gram_a * gram_c)

        finish(mb_got.at[sweep], 7, mb_sem.at[sweep, 1])
        packed = total(mb_got.at[sweep], 8)
        m_b = jnp.concatenate([packed[:, :64], packed[:, 64:]], axis=0) / scale_a
        solved_b = exact(inverse_b, m_b, NN)

        gram_src[sweep + 1] = pack_square(exact(solved_b, solved_b, NT))
        to_col(gram_src.at[sweep + 1], gram_got.at[sweep + 1], gram_sem.at[sweep + 1])
        gram_got[sweep + 1, col] = gram_src[sweep + 1]

        widen(solved_b / scale_a)

        def product_c(pair, acc):
            r = y[pair]
            return acc + r[:, :128] * wide_b[2 * pair] + r[:, 128:] * wide_b[2 * pair + 1]

        part = lax.fori_loop(0, 32, product_c, jnp.zeros((32, 128), F32), unroll=4)
        for piece in range(8):
            mc_src[sweep, piece] = part[4 * piece : 4 * piece + 4]
        to_row(lambda there: mc_src.at[sweep, there], mc_got.at[sweep], mc_sem.at[sweep])
        mc_got[sweep, row] = mc_src[sweep, row]
        finish(mc_got.at[sweep], 7, mc_sem.at[sweep, 1])
        mc_mid[sweep] = total(mc_got.at[sweep], 8)
        to_col(mc_mid.at[sweep], mc_col.at[sweep], mcc_sem.at[sweep])
        mc_col[sweep, col] = mc_mid[sweep]

        finish(gram_got.at[sweep + 1], 31, gram_sem.at[sweep + 1, 1])
        scale_b, gram_b = scales_of(unpack_square(total(gram_got.at[sweep + 1], 32)), total_j)
        inverse_c = inverse(gram_a * gram_b)

        finish(mc_col.at[sweep], 31, mcc_sem.at[sweep, 1])
        mc_sum[sweep] = total(mc_col.at[sweep], 32)
        to_row(lambda there: mc_sum.at[sweep], mc_all.at[sweep], mcr_sem.at[sweep])
        mc_all[sweep, row] = mc_sum[sweep]
        finish(mc_all.at[sweep], 7, mcr_sem.at[sweep, 1])
        m_c = jnp.concatenate([mc_all[sweep, piece] for piece in range(8)], axis=0) / scale_b
        solved_c = exact(inverse_c, m_c, NN)
        weights = jnp.sqrt(
            jnp.sum(solved_c * solved_c, axis=1, keepdims=True) / 128.0 + EPSILON
        )
        ct = solved_c / weights
        if sweep < SWEEPS - 1:
            gram_c = exact(ct, ct, NT)
            khatri_rao(ct * (scale_a / scale_b))
        else:
            a_out[...] = solved_a / scale_a
            b_out[...] = solved_b / scale_b
            c_out[...] = ct
            w_out[...] = weights

    for got, count, sem in sent:
        finish(got, count, sem)


def shards(total_i, total_j, tensor, factor_b0, factor_c0):
    vmem = pl.BlockSpec(memory_space=pltpu.VMEM)
    dma = pltpu.SemaphoreType.DMA
    n = SWEEPS

    def buffer(*shape):
        return pltpu.VMEM(shape, F32)

    a_t, b_t, c_t, w_t = pl.pallas_call(
        functools.partial(kernel, float(total_i), float(total_j)),
        out_shape=[
            jax.ShapeDtypeStruct((32, 256), F32),
            jax.ShapeDtypeStruct((32, 64), F32),
            jax.ShapeDtypeStruct((32, 128), F32),
            jax.ShapeDtypeStruct((32, 1), F32),
        ],
        in_specs=[pl.BlockSpec(memory_space=pl.ANY), vmem, vmem],
        out_specs=[vmem] * 4,
        scratch_shapes=[
            buffer(64, 256, 128),
            pltpu.VMEM((32, 256, 256), BF16),
            pltpu.VMEM((32, 256, 256), BF16),
            buffer(64, 32, 128),
            pltpu.VMEM((32, 64, 256), BF16),
            buffer(32, 32, 256),
            buffer(n + 1, 8, 128), buffer(n + 1, 32, 8, 128),
            buffer(n, 8, 8, 128), buffer(n, 32, 8, 128), buffer(n, 8, 128), buffer(n, 8, 8, 128),
            buffer(n, 8, 128), buffer(n, 8, 8, 128), buffer(n, 16, 128), buffer(n, 8, 16, 128),
            buffer(n, 8, 4, 128), buffer(n, 8, 4, 128), buffer(n, 4, 128),
            buffer(n, 32, 4, 128), buffer(n, 4, 128), buffer(n, 8, 4, 128),
            dma((8,)), dma((n + 1, 2)), dma((n, 2)), dma((n, 2)), dma((n, 2)), dma((n, 2)),
            dma((n, 2)), dma((n, 2)), dma((n, 2)),
        ],
        compiler_params=pltpu.CompilerParams(
            collective_id=0, has_side_effects=True, vmem_limit_bytes=48 * 2**20
        ),
    )(tensor, factor_b0.T, factor_c0.T)
    return a_t.T, b_t.T, c_t.T, w_t[:, 0]


def solution(mesh):
    total_i = 256 * mesh.shape["row"]
    total_j = 64 * mesh.shape["col"]
    return jax.shard_map(
        functools.partial(shards, total_i, total_j),
        mesh=mesh,
        in_specs=(P("row", "col", None), P("col", None), P()),
        out_specs=(P("row", None), P("col", None), P(), P()),
        check_vma=False,
    )
```

time: 1140 us -> 97.1 us (0.09)
  blocking collectives: 1020 us -> 0 us
  Pallas kernels: 0 us -> 92.4 us
  matrix products: 48.9 us -> 0 us
  other arithmetic: 40.7 us -> 0.63 us
  local copies, waits for them, and re-layouts: 21.9 us -> 3.25 us
    psum x7 -> x0, blocking collectives: 646 us -> none  [the longest x2 229 us: one_sweep(): moments = lax.psum(cross_gram(solved, solved), ('row', 'col'))]
    while x4 -> x0, blocking collectives: 285 us -> none
    pallas_call x0 -> x1, Pallas kernels: none -> 92.4 us  [shards(): pl.pallas_call(functools.partial(kernel, float(total_i), float(total_j)),...]
    all_gather x4 -> x0, blocking collectives: 90.7 us -> none  [the longest x2 63.9 us: one_sweep(): lax.all_gather(solved / scales[None, :], 'col', axis=0, tiled=True)]
    dot_general x14 -> x0, matrix products: 46.7 us -> none  [the longest x2 26.5 us: one_sweep(): jnp.einsum('ijk,jr->irk', tensor, b_block, precision=lax.Precision.HIGHEST)]
    another operation x30 -> x0, other arithmetic: 40.1 us -> none  [the longest x18 21.6 us: solve_rows(): cholesky_low = jnp.linalg.cholesky(system)]
    while x15 -> x0, local copies, waits for them, and re-layouts: 15.2 us -> none  [the longest x3 12.3 us: shards(): lax.fori_loop(0, SWEEPS, one_sweep, start)]
where the time goes in v1:
time: 97.1 us; the launch traced here: 96.9 us
  Pallas kernels  92.4 us (95%)
  local copies, waits for them, and re-layouts  3.25 us (3%)
    pallas_call x1, Pallas kernels, shards(): pl.pallas_call(functools.partial(kernel, float(total_i), float(total_j)),...  92.4 us
    unnamed x7, local copies, waits for them, and re-layouts  3.25 us

profile of v1, /device:TPU:1, one launch (start us, length us, event | category | flops | bytes accessed | tf_op | source)
XLA Modules:
  0.0 96.9 jit_solution(818903995946960167)
XLA Ops:
  0.6 0.0 copy-start
  0.6 0.7 copy-done
  1.3 0.0 copy-start.1
  1.4 0.7 copy-done.1
  2.1 92.4 %shard_map.66 = (f32[32,256]{1,0:T(8,128)S(1)}, f32[32,64]{1,0:T(8,128)S(1)}, f32[32,128]{1,0:T(8,128)S(1)}, f32[32,1]{1,0:T(8,128)S(1)}) custom-call(f32[256,64,128]{2,1,0:T(8,128)} %tensor.1, f32[32,64]{1,0:T(8,128)S(1)} %bitcast.6, f32[32,128]{1,0:T(8,128)S(1)} %bitcast.7), custom_call_target="tpu_custom_call" | custom-call | tf_op jit(solution)/shard_map/pallas_call | solution.py:333
  94.4 0.6 reduce
  95.1 0.6 copy.10
  95.7 0.6 copy.11
  96.3 0.6 copy.12
Async XLA Ops:
  0.6 0.7 copy-start
  1.3 0.7 copy-start.1

commit v2 on v1

v2 whole, which is shorter than its diff:
```python
import functools

import jax
import jax.numpy as jnp
from jax import lax
from jax.experimental import pallas as pl
from jax.experimental.pallas import tpu as pltpu
from jax.sharding import PartitionSpec as P

SWEEPS = 2
FIRST = 3
EPSILON = 1e-06
F32 = jnp.float32
BF16 = jnp.bfloat16
MESH = pl.DeviceIdType.MESH
NT = (((1,), (1,)), ((), ()))
NN = (((1,), (0,)), ((), ()))
TN = (((0,), (0,)), ((), ()))


def exact(left, right, dims):
    return lax.dot_general(
        left, right, dims, precision=lax.Precision.HIGHEST, preferred_element_type=F32
    )


def fast(left, right, dims):
    return lax.dot_general(left, right, dims, preferred_element_type=F32)


def split(x):
    high = x.astype(BF16)
    return high, (x - high.astype(F32)).astype(BF16)


def far_first(at, ring):
    odd = lax.rem(at, 2)
    return lax.rem(ring // 2 + lax.div(at + 1, 2) * (2 * odd - 1) + ring, ring)


def pack_square(g):
    return jnp.concatenate([g[8 * q : 8 * q + 8, :] for q in range(4)], axis=1)


def unpack_square(p):
    return jnp.concatenate([p[:, 32 * q : 32 * q + 32] for q in range(4)], axis=0)


def lanes(x, at):
    return jnp.broadcast_to(x[:, at : at + 1], (8, 128))


def sublanes(x, at):
    return jnp.broadcast_to(x[at : at + 1, :], (8, 128))


def inverse(system):
    row = lax.broadcasted_iota(jnp.int32, (32, 128), 0)
    lane = lax.broadcasted_iota(jnp.int32, (32, 128), 1)
    unit = jnp.where(lane == row + 32, 1.0, 0.0).astype(F32)
    wide = jnp.concatenate([system, jnp.zeros((32, 96), F32)], axis=1) + unit
    parts = [wide[8 * q : 8 * q + 8] for q in range(4)]
    sub = lax.broadcasted_iota(jnp.int32, (8, 128), 0)
    out = []
    for q in range(4):
        cols = [[lanes(parts[t], 8 * q + c) for t in range(q, 4)] for c in range(8)]
        rows = [sublanes(parts[q], c) for c in range(8)]
        small = [[sublanes(cols[b][0], a) if a >= b else None for b in range(8)] for a in range(8)]
        done = jnp.zeros((8, 128), F32)
        for c in range(8):
            pivot = small[c][c]
            over = 1.0 / pivot
            low = [small[a][c] * over if a > c else None for a in range(8)]
            for a in range(c + 1, 8):
                for b in range(c + 1, a + 1):
                    small[a][b] = small[a][b] - low[a] * small[b][c]
            for a in range(c + 1, 8):
                rows[a] = rows[a] - low[a] * rows[c]
            for t in range(1, 4 - q):
                step = cols[c][t] * over
                for b in range(c + 1, 8):
                    cols[b][t] = cols[b][t] - step * small[b][c]
                parts[q + t] = parts[q + t] - step * rows[c]
            done = jnp.where(sub == c, rows[c] * lax.rsqrt(pivot), done)
        out.append(done)
    w = jnp.concatenate(out, axis=0)[:, 32:64]
    return exact(w, w, TN)


def lane_sums(leaf, first, bits):
    if bits == 0:
        return leaf(first)
    bit = bits - 1
    left = lane_sums(leaf, first, bit)
    right = lane_sums(leaf, first + 2**bit, bit)
    at = lax.broadcasted_iota(jnp.int32, left.shape, 1)
    even = (at & 2**bit) == 0
    moved = pltpu.roll(jnp.where(even, right, left), 128 - 2**bit, 1)
    return jnp.where(even, left, right) + moved


def scales_of(moments, count):
    row = lax.broadcasted_iota(jnp.int32, (32, 32), 0)
    lane = lax.broadcasted_iota(jnp.int32, (32, 32), 1)
    diagonal = jnp.where(row == lane, moments, 0.0)
    down = jnp.sqrt(jnp.sum(diagonal, axis=1, keepdims=True) / count + EPSILON)
    across = jnp.sqrt(jnp.sum(diagonal, axis=0, keepdims=True) / count + EPSILON)
    return down, moments / (down * across)


def kernel(
    total_i, total_j,
    tensor, b_in, c_in,
    a_out, b_out, c_out, w_out,
    b_here, c_here, staged, high, low, wide_b, kr, u, y,
    gram_src, gram_got, ma_src, ma_got, ma_sum, ma_all,
    mom_src, mom_got, mb_src, mb_got,
    mc_src, mc_got, mc_mid, mc_all,
    in_sem, load_sem, gram_sem, ma_sem, maz_sem, mom_sem, mb_sem, mc_sem, mcc_sem,
):
    row, col = lax.axis_index("row"), lax.axis_index("col")
    z, y_at = lax.div(col, 4), lax.rem(col, 4)
    x_at, core = lax.div(row, 2), lax.rem(row, 2)
    place, quarter = 4 * row + y_at, lax.rem(row, 4)
    mine = 2 * y_at + lax.rem(z, 2)
    copy_b = pltpu.make_async_copy(b_in, b_here, in_sem.at[0])
    copy_c = pltpu.make_async_copy(c_in, c_here, in_sem.at[1])
    copy_b.start()
    copy_c.start()

    def load(j, carry):
        pltpu.make_async_copy(tensor.at[:, j, :], staged.at[j], load_sem.at[j // 8]).start()
        return carry

    lax.fori_loop(0, 64, load, 0)

    barrier = pltpu.get_barrier_semaphore()

    ys = [4 * z + lax.rem(y_at + off, 4) for off in (2, 3, 1, 0)]
    y_offs = [lax.rem(y_at + off, 4) for off in (2, 3, 1, 0)]

    def each_col(act):
        def some(step, carry):
            base = 4 * lax.rem(z + far_first(step, 8), 8)
            for off in y_offs:
                act(base + off)
            return carry

        lax.fori_loop(0, 7, some, 0)
        for there in ys[:3]:
            act(there)

    def each_plane(act):
        def some(step, carry):
            base = 2 * lax.rem(x_at + far_first(step, 4), 4)
            for there in ys:
                act(base + 1 - core, there)
                act(base + core, there)
            return carry

        lax.fori_loop(0, 3, some, 0)
        for there in ys[:3]:
            act(2 * x_at + 1 - core, there)
            act(row, there)
        act(2 * x_at + 1 - core, ys[3])

    def greet(there_row, there_col):
        pl.semaphore_signal(
            barrier, inc=1, device_id=(there_row, there_col), device_id_type=MESH
        )

    each_col(lambda there: greet(row, there))
    each_plane(greet)

    sent = []

    def finish(got, count, sem):
        view = got.at[pl.ds(0, count)]
        pltpu.make_async_copy(view, view, sem).wait()

    def send(source, got, slot, device, sems):
        pltpu.make_async_remote_copy(
            src_ref=source, dst_ref=got.at[slot], send_sem=sems.at[0], recv_sem=sems.at[1],
            device_id=device, device_id_type=MESH,
        ).start()

    def to_col(pick, got, sems):
        each_col(lambda there: send(pick(there), got, col, (row, there), sems))
        sent.append((got, 31, sems.at[0]))

    def to_plane(pick, got, sems):
        each_plane(lambda *there: send(pick(there), got, place, there, sems))
        sent.append((got, 31, sems.at[0]))

    def to_row(source, got, sems):
        def one(step, carry):
            send(source, got, row, (lax.rem(row + step, 8), col), sems)
            return carry

        lax.fori_loop(1, 8, one, 0)
        sent.append((got, 7, sems.at[0]))

    def to_tiles(source, got, sems):
        def one(step, carry):
            tile = lax.rem(mine + step, 8)
            there = 4 * (2 * lax.div(z, 2) + lax.rem(tile, 2)) + lax.div(tile, 2)
            send(source, got, mine, (row, there), sems)
            return carry

        lax.fori_loop(1, 8, one, 0)
        sent.append((got, 7, sems.at[0]))

    def to_quarters(source, got, sems):
        rows = [4 * lax.div(row, 4) + lax.rem(quarter + off, 4) for off in (2, 1, 3, 0)]

        def some(step, carry):
            there = 4 * lax.rem(z + far_first(step, 8), 8) + y_at
            for there_row in rows:
                send(source, got, 8 * quarter + z, (there_row, there), sems)
            return carry

        lax.fori_loop(0, 7, some, 0)
        for there_row in rows[:3]:
            send(source, got, 8 * quarter + z, (there_row, col), sems)
        sent.append((got, 31, sems.at[0]))

    def total(got, count):
        acc = got[0]
        for at in range(1, count):
            acc = acc + got[at]
        return acc
    copy_b.wait()
    copy_c.wait()
    bt = b_here[...]
    ct = c_here[...]
    gram_c = exact(ct, ct, NT)
    gram_src[0] = pack_square(exact(bt, bt, NT))

    def widen(values):
        for j in range(64):
            wide_b[j] = jnp.broadcast_to(values[:, j : j + 1], (32, 128))

    def khatri_rao(third):
        def body(pair, carry):
            h, l = split(
                jnp.concatenate([wide_b[2 * pair] * third, wide_b[2 * pair + 1] * third], axis=1)
            )
            kr[pair, 0:32, :] = h
            kr[pair, 32:64, :] = l
            return carry

        lax.fori_loop(0, 32, body, 0)

    widen(bt)
    khatri_rao(ct)

    def product_a(pair, acc):
        p = fast(kr[pair], high[pair], NT)
        q = fast(kr[pair, 0:32, :], low[pair], NT)
        return acc + (p[:32] + p[32:] + q)

    def unpack(group, acc):
        view = staged.at[pl.ds(8 * group, 8)]
        pltpu.make_async_copy(view, view, load_sem.at[group]).wait()
        for at in range(4):
            pair = 4 * group + at
            h, l = split(jnp.concatenate([staged[2 * pair], staged[2 * pair + 1]], axis=1))
            high[pair] = h
            low[pair] = l
            acc = product_a(pair, acc)
        return acc

    gram_a = None
    for sweep in range(SWEEPS):
        if sweep == 0:
            part = lax.fori_loop(0, FIRST, unpack, jnp.zeros((32, 256), F32))
            pl.semaphore_wait(barrier, 62)
            to_col(lambda there: gram_src.at[0], gram_got.at[0], gram_sem.at[0])
            gram_got[0, col] = gram_src[0]
            part = lax.fori_loop(FIRST, 8, unpack, part)
        else:
            part = lax.fori_loop(0, 32, product_a, jnp.zeros((32, 256), F32), unroll=4)
        for tile in range(8):
            q, half = divmod(tile, 2)
            ma_src[sweep, tile] = part[8 * q : 8 * q + 8, 128 * half : 128 * half + 128]

        def tile_of(there):
            tile = 2 * lax.rem(there, 4) + lax.rem(lax.div(there, 4), 2)
            return ma_src.at[sweep, tile]

        to_col(tile_of, ma_got.at[sweep], ma_sem.at[sweep])
        ma_got[sweep, col] = ma_src[sweep, mine]

        c_high, c_low = split(ct)
        none = jnp.zeros((32, 128), BF16)

        def twice(x):
            return jnp.concatenate(
                [jnp.concatenate([x, none], axis=1), jnp.concatenate([none, x], axis=1)], axis=0
            )

        c_high = twice(c_high)
        c_both = jnp.concatenate([c_high, twice(c_low)], axis=0)

        def product_u(pair, carry):
            p = fast(c_both, high[pair], NT)
            q = fast(c_high, low[pair], NT)
            u[pair] = p[:64] + p[64:] + q
            return carry

        lax.fori_loop(0, 32, product_u, 0, unroll=4)
        if sweep == 0:
            finish(gram_got.at[0], 31, gram_sem.at[0, 1])
            gram_b = unpack_square(total(gram_got.at[0], 32))
        inverse_a = inverse(gram_b * gram_c)
        finish(ma_got.at[sweep], 31, ma_sem.at[sweep, 1])
        summed = total(ma_got.at[sweep], 32)
        ma_sum[sweep] = summed

        to_tiles(ma_sum.at[sweep], ma_all.at[sweep], maz_sem.at[sweep])
        ma_all[sweep, mine] = summed
        finish(ma_all.at[sweep], 7, maz_sem.at[sweep, 1])
        m_a = jnp.concatenate(
            [
                jnp.concatenate([ma_all[sweep, 2 * q], ma_all[sweep, 2 * q + 1]], axis=1)
                for q in range(4)
            ],
            axis=0,
        )
        solved_a = exact(inverse_a, m_a, NN)

        mom_src[sweep] = pack_square(exact(solved_a, solved_a, NT))
        to_row(mom_src.at[sweep], mom_got.at[sweep], mom_sem.at[sweep])
        mom_got[sweep, row] = mom_src[sweep]
        def leaf(j):
            pair, at = divmod(j, 2)
            r = u[pair, 32 * at : 32 * at + 32, :] * solved_a
            return r[:, :128] + r[:, 128:]

        part = lane_sums(leaf, 0, 6)
        part = part + pltpu.roll(part, 64, 1)
        lane = lax.broadcasted_iota(jnp.int32, (16, 128), 1)
        mb_src[sweep] = jnp.where(lane < 64, part[:16], part[16:])
        to_row(mb_src.at[sweep], mb_got.at[sweep], mb_sem.at[sweep])
        mb_got[sweep, row] = mb_src[sweep]

        a_high, a_low = split(solved_a)
        a_both = jnp.concatenate([a_high, a_low], axis=0)

        def product_y(pair, carry):
            p = fast(a_both, high[pair], NN)
            q = fast(a_high, low[pair], NN)
            y[pair] = p[:32] + p[32:] + q
            return carry

        lax.fori_loop(0, 32, product_y, 0, unroll=4)
        finish(mom_got.at[sweep], 7, mom_sem.at[sweep, 1])
        scale_a, gram_a = scales_of(unpack_square(total(mom_got.at[sweep], 8)), total_i)
        inverse_b = inverse(gram_a * gram_c)
        finish(mb_got.at[sweep], 7, mb_sem.at[sweep, 1])
        packed = total(mb_got.at[sweep], 8)
        m_b = jnp.concatenate([packed[:, :64], packed[:, 64:]], axis=0) / scale_a
        solved_b = exact(inverse_b, m_b, NN)

        widen(solved_b / scale_a)

        def product_c(pair, acc):
            r = y[pair]
            return acc + r[:, :128] * wide_b[2 * pair] + r[:, 128:] * wide_b[2 * pair + 1]

        part = lax.fori_loop(0, 32, product_c, jnp.zeros((32, 128), F32), unroll=4)
        for piece in range(4):
            mc_src[sweep, piece] = part[8 * piece : 8 * piece + 8]
        to_plane(
            lambda there: mc_src.at[sweep, lax.rem(there[0], 4)], mc_got.at[sweep], mc_sem.at[sweep]
        )
        mc_got[sweep, place] = mc_src[sweep, quarter]
        gram_src[sweep + 1] = pack_square(exact(solved_b, solved_b, NT))
        to_col(lambda there: gram_src.at[sweep + 1], gram_got.at[sweep + 1], gram_sem.at[sweep + 1])
        gram_got[sweep + 1, col] = gram_src[sweep + 1]
        finish(mc_got.at[sweep], 31, mc_sem.at[sweep, 1])
        mc_mid[sweep] = total(mc_got.at[sweep], 32)
        to_quarters(mc_mid.at[sweep], mc_all.at[sweep], mcc_sem.at[sweep])
        mc_all[sweep, 8 * quarter + z] = mc_mid[sweep]

        finish(gram_got.at[sweep + 1], 31, gram_sem.at[sweep + 1, 1])
        scale_b, gram_b = scales_of(unpack_square(total(gram_got.at[sweep + 1], 32)), total_j)
        inverse_c = inverse(gram_a * gram_b)
        finish(mc_all.at[sweep], 31, mcc_sem.at[sweep, 1])
        m_c = jnp.concatenate([total(mc_all.at[sweep, pl.ds(8 * piece, 8)], 8) for piece in range(4)], axis=0) / scale_b
        solved_c = exact(inverse_c, m_c, NN)
        weights = jnp.sqrt(
            jnp.sum(solved_c * solved_c, axis=1, keepdims=True) / 128.0 + EPSILON
        )
        ct = solved_c / weights
        if sweep < SWEEPS - 1:
            gram_c = exact(ct, ct, NT)
            khatri_rao(ct * (scale_a / scale_b))
        else:
            a_out[...] = solved_a / scale_a
            b_out[...] = solved_b / scale_b
            c_out[...] = ct
            at = lax.broadcasted_iota(jnp.int32, (32, 32), 0)
            unit = at == lax.broadcasted_iota(jnp.int32, (32, 32), 1)
            w_out[...] = jnp.sum(jnp.where(unit, weights, 0.0), axis=0, keepdims=True)
    for got, count, sem in sent:
        finish(got, count, sem)


def shards(total_i, total_j, tensor, factor_b0, factor_c0):
    vmem = pl.BlockSpec(memory_space=pltpu.VMEM)
    dma = pltpu.SemaphoreType.DMA
    n = SWEEPS

    def buffer(*shape):
        return pltpu.VMEM(shape, F32)

    results = [
        jax.ShapeDtypeStruct((32, 256), F32),
        jax.ShapeDtypeStruct((32, 64), F32),
        jax.ShapeDtypeStruct((32, 128), F32),
        jax.ShapeDtypeStruct((1, 32), F32),
    ]
    a_t, b_t, c_t, w_t = pl.pallas_call(
        functools.partial(kernel, float(total_i), float(total_j)),
        out_shape=results,
        in_specs=[pl.BlockSpec(memory_space=pltpu.HBM)] * 3,
        out_specs=[vmem] * 4,
        scratch_shapes=[
            buffer(32, 64), buffer(32, 128),
            buffer(64, 256, 128),
            pltpu.VMEM((32, 256, 256), BF16),
            pltpu.VMEM((32, 256, 256), BF16),
            buffer(64, 32, 128),
            pltpu.VMEM((32, 64, 256), BF16),
            buffer(32, 64, 256),
            buffer(32, 32, 256),
            buffer(n + 1, 8, 128), buffer(n + 1, 32, 8, 128),
            buffer(n, 8, 8, 128), buffer(n, 32, 8, 128), buffer(n, 8, 128), buffer(n, 8, 8, 128),
            buffer(n, 8, 128), buffer(n, 8, 8, 128), buffer(n, 16, 128), buffer(n, 8, 16, 128),
            buffer(n, 4, 8, 128), buffer(n, 32, 8, 128), buffer(n, 8, 128),
            buffer(n, 32, 8, 128),
            dma((2,)), dma((8,)), dma((n + 1, 2)), dma((n, 2)), dma((n, 2)), dma((n, 2)), dma((n, 2)),
            dma((n, 2)), dma((n, 2)),
        ],
        compiler_params=pltpu.CompilerParams(
            collective_id=0, has_side_effects=True, vmem_limit_bytes=48 * 2**20
        ),
    )(
        tensor,
        pltpu.with_memory_space_constraint(factor_b0.T, pltpu.HBM),
        pltpu.with_memory_space_constraint(factor_c0.T, pltpu.HBM),
    )
    return a_t.T, b_t.T, c_t.T, w_t[0]


def solution(mesh):
    total_i = 256 * mesh.shape["row"]
    total_j = 64 * mesh.shape["col"]
    return jax.shard_map(
        functools.partial(shards, total_i, total_j),
        mesh=mesh,
        in_specs=(P("row", "col", None), P("col", None), P()),
        out_specs=(P("row", None), P("col", None), P(), P()),
        check_vma=False,
    )
```

time: 97.1 us -> 77.2 us (0.80)
  Pallas kernels: 92.4 us -> 74.2 us
    pallas_call x1, Pallas kernels: 92.4 us -> 74.2 us  [shards(): pl.pallas_call(functools.partial(kernel, float(total_i), float(total_j)),...]
    unnamed x7 -> x4, local copies, waits for them, and re-layouts: 3.25 us -> 2.34 us
where the time goes in v2:
time: 77.2 us; the launch traced here: 77.1 us
  Pallas kernels  74.2 us (96%)
  local copies, waits for them, and re-layouts  2.34 us (3%)
    pallas_call x1, Pallas kernels, shards(): pl.pallas_call(functools.partial(kernel, float(total_i), float(total_j)),...  74.2 us
    unnamed x4, local copies, waits for them, and re-layouts  2.34 us

profile of v2, /device:TPU:1, one launch (start us, length us, event | category | flops | bytes accessed | tf_op | source)
XLA Modules:
  0.0 77.1 jit_solution(7897856186087772801)
XLA Ops:
  0.6 74.2 %shard_map.66 = (f32[32,256]{1,0:T(8,128)S(1)}, f32[32,64]{1,0:T(8,128)S(1)}, f32[32,128]{1,0:T(8,128)S(1)}, f32[1,32]{1,0:T(1,128)S(1)}) custom-call(f32[256,64,128]{2,1,0:T(8,128)} %tensor.1, f32[32,64]{1,0:T(8,128)} %bitcast.10, f32[32,128]{1,0:T(8,128)} %bitcast.11), custom_call_target="tpu_custom_call" | custom-call | tf_op jit(solution)/shard_map/pallas_call | solution.py:424
  74.8 0.6 copy.11
  75.4 0.6 copy.12
  76.0 0.6 copy.13
  76.6 0.5 copy.14

commit v3 on v2

--- a/solution.py
+++ b/solution.py
@@ -9,6 +9,7 @@
 
 SWEEPS = 2
 FIRST = 3
+TURNS = (20, 26, 8)
 EPSILON = 1e-06
 F32 = jnp.float32
 BF16 = jnp.bfloat16
@@ -112,7 +113,7 @@
     total_i, total_j,
     tensor, b_in, c_in,
     a_out, b_out, c_out, w_out,
-    b_here, c_here, staged, high, low, wide_b, kr, u, y,
+    b_here, c_here, staged, high, low, wide_b, kr, u, y, turned_high, turned_low, chooser, zed,
     gram_src, gram_got, ma_src, ma_got, ma_sum, ma_all,
     mom_src, mom_got, mb_src, mb_got,
     mc_src, mc_got, mc_mid, mc_all,
@@ -132,7 +133,7 @@
         pltpu.make_async_copy(tensor.at[:, j, :], staged.at[j], load_sem.at[j // 8]).start()
         return carry
 
-    lax.fori_loop(0, 64, load, 0)
+    lax.fori_loop(0, 16, load, 0)
 
     barrier = pltpu.get_barrier_semaphore()
 
@@ -171,6 +172,7 @@
 
     each_col(lambda there: greet(row, there))
     each_plane(greet)
+    lax.fori_loop(16, 64, load, 0)
 
     sent = []
 
@@ -259,6 +261,46 @@
         q = fast(kr[pair, 0:32, :], low[pair], NT)
         return acc + (p[:32] + p[32:] + q)
 
+    def turn(pair, carry):
+        first, second = staged[2 * pair].T, staged[2 * pair + 1].T
+        at = pl.multiple_of(16 * lax.rem(pair, 16), 16)
+        for k8 in range(16):
+            rows = slice(8 * k8, 8 * k8 + 8)
+            h, l = split(jnp.concatenate([first[rows], second[rows]], axis=0))
+            turned_high[k8, lax.div(pair, 16), pl.ds(at, 16), :] = h
+            turned_low[k8, lax.div(pair, 16), pl.ds(at, 16), :] = l
+        return carry
+
+    def spread(values):
+        lane = lax.broadcasted_iota(jnp.int32, (32, 256), 1)
+        row = lax.broadcasted_iota(jnp.int32, (32, 256), 0)
+        repeat = jnp.where(lax.div(lane, 8) == row, 1.0, 0.0).astype(F32)
+        for half in range(2):
+            wide = exact(values[:, 32 * half : 32 * half + 32], repeat, NN)
+            for k in range(8):
+                h, l = split(jnp.where(lax.rem(lane, 8) == k, wide, 0.0))
+                chooser[half, 32 * k : 32 * k + 32, :] = h
+                chooser[half, 256 + 32 * k : 256 + 32 * k + 32, :] = l
+
+    def product_z(k8, carry):
+        acc = None
+        for half in range(2):
+            p = fast(chooser[half], turned_high[k8, half], NN)
+            q = fast(chooser[half, 0:256, :], turned_low[k8, half], NN)
+            r = p[:256] + p[256:] + q
+            acc = r if acc is None else acc + r
+        zed[k8] = acc
+        return carry
+
+    def contract_z(third):
+        acc = jnp.zeros((32, 256), F32)
+        for k in range(128):
+            k8, at = divmod(k, 8)
+            factor = jnp.broadcast_to(third[:, k : k + 1], (32, 128))
+            r = zed[k8, 32 * at : 32 * at + 32, :]
+            acc = acc + r * jnp.concatenate([factor, factor], axis=1)
+        return acc
+
     def unpack(group, acc):
         view = staged.at[pl.ds(8 * group, 8)]
         pltpu.make_async_copy(view, view, load_sem.at[group]).wait()
@@ -279,7 +321,7 @@
             gram_got[0, col] = gram_src[0]
             part = lax.fori_loop(FIRST, 8, unpack, part)
         else:
-            part = lax.fori_loop(0, 32, product_a, jnp.zeros((32, 256), F32), unroll=4)
+            part = contract_z(ct * (scale_a / scale_b))
         for tile in range(8):
             q, half = divmod(tile, 2)
             ma_src[sweep, tile] = part[8 * q : 8 * q + 8, 128 * half : 128 * half + 128]
@@ -319,6 +361,8 @@
 
         to_tiles(ma_sum.at[sweep], ma_all.at[sweep], maz_sem.at[sweep])
         ma_all[sweep, mine] = summed
+        if sweep == 0:
+            lax.fori_loop(0, TURNS[0], turn, 0, unroll=2)
         finish(ma_all.at[sweep], 7, maz_sem.at[sweep, 1])
         m_a = jnp.concatenate(
             [
@@ -354,6 +398,8 @@
             return carry
 
         lax.fori_loop(0, 32, product_y, 0, unroll=4)
+        if sweep == 0:
+            lax.fori_loop(TURNS[0], TURNS[1], turn, 0, unroll=2)
         finish(mom_got.at[sweep], 7, mom_sem.at[sweep, 1])
         scale_a, gram_a = scales_of(unpack_square(total(mom_got.at[sweep], 8)), total_i)
         inverse_b = inverse(gram_a * gram_c)
@@ -378,11 +424,17 @@
         gram_src[sweep + 1] = pack_square(exact(solved_b, solved_b, NT))
         to_col(lambda there: gram_src.at[sweep + 1], gram_got.at[sweep + 1], gram_sem.at[sweep + 1])
         gram_got[sweep + 1, col] = gram_src[sweep + 1]
+        if sweep == 0:
+            lax.fori_loop(TURNS[1], 32, turn, 0, unroll=2)
+            spread(solved_b / scale_a)
+            lax.fori_loop(0, TURNS[2], product_z, 0, unroll=2)
         finish(mc_got.at[sweep], 31, mc_sem.at[sweep, 1])
         mc_mid[sweep] = total(mc_got.at[sweep], 32)
         to_quarters(mc_mid.at[sweep], mc_all.at[sweep], mcc_sem.at[sweep])
         mc_all[sweep, 8 * quarter + z] = mc_mid[sweep]
 
+        if sweep == 0:
+            lax.fori_loop(TURNS[2], 16, product_z, 0, unroll=2)
         finish(gram_got.at[sweep + 1], 31, gram_sem.at[sweep + 1, 1])
         scale_b, gram_b = scales_of(unpack_square(total(gram_got.at[sweep + 1], 32)), total_j)
         inverse_c = inverse(gram_a * gram_b)
@@ -395,7 +447,6 @@
         ct = solved_c / weights
         if sweep < SWEEPS - 1:
             gram_c = exact(ct, ct, NT)
-            khatri_rao(ct * (scale_a / scale_b))
         else:
             a_out[...] = solved_a / scale_a
             b_out[...] = solved_b / scale_b
@@ -435,6 +486,10 @@
             pltpu.VMEM((32, 64, 256), BF16),
             buffer(32, 64, 256),
             buffer(32, 32, 256),
+            pltpu.VMEM((16, 2, 256, 256), BF16),
+            pltpu.VMEM((16, 2, 256, 256), BF16),
+            pltpu.VMEM((2, 512, 256), BF16),
+            buffer(16, 256, 256),
             buffer(n + 1, 8, 128), buffer(n + 1, 32, 8, 128),
             buffer(n, 8, 8, 128), buffer(n, 32, 8, 128), buffer(n, 8, 128), buffer(n, 8, 8, 128),
             buffer(n, 8, 128), buffer(n, 8, 8, 128), buffer(n, 16, 128), buffer(n, 8, 16, 128),

time: 77.2 us -> 73.8 us (0.956)
  Pallas kernels: 74.2 us -> 70.7 us
    pallas_call x1, Pallas kernels: 74.2 us -> 70.7 us  [shards(): pl.pallas_call(functools.partial(kernel, float(total_i), float(total_j)),...]
where the time goes in v3:
time: 73.8 us; the launch traced here: 73.7 us
  Pallas kernels  70.7 us (96%)
  local copies, waits for them, and re-layouts  2.34 us (3%)
    pallas_call x1, Pallas kernels, shards(): pl.pallas_call(functools.partial(kernel, float(total_i), float(total_j)),...  70.7 us
    unnamed x4, local copies, waits for them, and re-layouts  2.34 us

profile of v3, /device:TPU:1, one launch (start us, length us, event | category | flops | bytes accessed | tf_op | source)
XLA Modules:
  0.0 73.7 jit_solution(6360281787172958853)
XLA Ops:
  0.6 70.7 %shard_map.66 = (f32[32,256]{1,0:T(8,128)S(1)}, f32[32,64]{1,0:T(8,128)S(1)}, f32[32,128]{1,0:T(8,128)S(1)}, f32[1,32]{1,0:T(1,128)S(1)}) custom-call(f32[256,64,128]{2,1,0:T(8,128)} %tensor.1, f32[32,64]{1,0:T(8,128)} %bitcast.10, f32[32,128]{1,0:T(8,128)} %bitcast.11), custom_call_target="tpu_custom_call" | custom-call | tf_op jit(solution)/shard_map/pallas_call | solution.py:475
  71.4 0.6 copy.11
  72.0 0.6 copy.12
  72.6 0.6 copy.13
  73.2 0.5 copy.14

commit v4 on v3

--- a/solution.py
+++ b/solution.py
@@ -8,7 +8,7 @@
 from jax.sharding import PartitionSpec as P
 
 SWEEPS = 2
-FIRST = 3
+FIRST = 4
 TURNS = (20, 26, 8)
 EPSILON = 1e-06
 F32 = jnp.float32
@@ -112,8 +112,8 @@
 def kernel(
     total_i, total_j,
     tensor, b_in, c_in,
-    a_out, b_out, c_out, w_out,
-    b_here, c_here, staged, high, low, wide_b, kr, u, y, turned_high, turned_low, chooser, zed,
+    out,
+    b_here, c_here, staged, high, low, u, y, turned_high, turned_low, chooser, zed,
     gram_src, gram_got, ma_src, ma_got, ma_sum, ma_all,
     mom_src, mom_got, mb_src, mb_got,
     mc_src, mc_got, mc_mid, mc_all,
@@ -235,32 +235,6 @@
     copy_c.wait()
     bt = b_here[...]
     ct = c_here[...]
-    gram_c = exact(ct, ct, NT)
-    gram_src[0] = pack_square(exact(bt, bt, NT))
-
-    def widen(values):
-        for j in range(64):
-            wide_b[j] = jnp.broadcast_to(values[:, j : j + 1], (32, 128))
-
-    def khatri_rao(third):
-        def body(pair, carry):
-            h, l = split(
-                jnp.concatenate([wide_b[2 * pair] * third, wide_b[2 * pair + 1] * third], axis=1)
-            )
-            kr[pair, 0:32, :] = h
-            kr[pair, 32:64, :] = l
-            return carry
-
-        lax.fori_loop(0, 32, body, 0)
-
-    widen(bt)
-    khatri_rao(ct)
-
-    def product_a(pair, acc):
-        p = fast(kr[pair], high[pair], NT)
-        q = fast(kr[pair, 0:32, :], low[pair], NT)
-        return acc + (p[:32] + p[32:] + q)
-
     def turn(pair, carry):
         first, second = staged[2 * pair].T, staged[2 * pair + 1].T
         at = pl.multiple_of(16 * lax.rem(pair, 16), 16)
@@ -301,25 +275,30 @@
             acc = acc + r * jnp.concatenate([factor, factor], axis=1)
         return acc
 
-    def unpack(group, acc):
-        view = staged.at[pl.ds(8 * group, 8)]
-        pltpu.make_async_copy(view, view, load_sem.at[group]).wait()
-        for at in range(4):
-            pair = 4 * group + at
-            h, l = split(jnp.concatenate([staged[2 * pair], staged[2 * pair + 1]], axis=1))
-            high[pair] = h
-            low[pair] = l
-            acc = product_a(pair, acc)
+    def first_product(groups, acc):
+        for group in groups:
+            view = staged.at[pl.ds(8 * group, 8)]
+            pltpu.make_async_copy(view, view, load_sem.at[group]).wait()
+            for pair in range(4 * group, 4 * group + 4):
+                h, l = split(jnp.concatenate([staged[2 * pair], staged[2 * pair + 1]], axis=1))
+                high[pair] = h
+                low[pair] = l
+                first = jnp.broadcast_to(bt[:, 2 * pair : 2 * pair + 1], (32, 128))
+                second = jnp.broadcast_to(bt[:, 2 * pair + 1 : 2 * pair + 2], (32, 128))
+                rows_h, rows_l = split(jnp.concatenate([first * ct, second * ct], axis=1))
+                p = fast(jnp.concatenate([rows_h, rows_l], axis=0), h, NT)
+                acc = acc + (p[:32] + p[32:] + fast(rows_h, l, NT))
         return acc
 
     gram_a = None
     for sweep in range(SWEEPS):
         if sweep == 0:
-            part = lax.fori_loop(0, FIRST, unpack, jnp.zeros((32, 256), F32))
+            part = first_product(range(FIRST), jnp.zeros((32, 256), F32))
+            gram_src[0] = pack_square(exact(bt, bt, NT))
             pl.semaphore_wait(barrier, 62)
             to_col(lambda there: gram_src.at[0], gram_got.at[0], gram_sem.at[0])
             gram_got[0, col] = gram_src[0]
-            part = lax.fori_loop(FIRST, 8, unpack, part)
+            part = first_product(range(FIRST, 8), part)
         else:
             part = contract_z(ct * (scale_a / scale_b))
         for tile in range(8):
@@ -333,6 +312,8 @@
         to_col(tile_of, ma_got.at[sweep], ma_sem.at[sweep])
         ma_got[sweep, col] = ma_src[sweep, mine]
 
+        if sweep == 0:
+            gram_c = exact(ct, ct, NT)
         c_high, c_low = split(ct)
         none = jnp.zeros((32, 128), BF16)
 
@@ -408,13 +389,11 @@
         m_b = jnp.concatenate([packed[:, :64], packed[:, 64:]], axis=0) / scale_a
         solved_b = exact(inverse_b, m_b, NN)
 
-        widen(solved_b / scale_a)
-
-        def product_c(pair, acc):
-            r = y[pair]
-            return acc + r[:, :128] * wide_b[2 * pair] + r[:, 128:] * wide_b[2 * pair + 1]
-
-        part = lax.fori_loop(0, 32, product_c, jnp.zeros((32, 128), F32), unroll=4)
+        rescaled_b = solved_b / scale_a
+        part = jnp.zeros((32, 128), F32)
+        for j in range(64):
+            r = y[j // 2, :, 128 * (j % 2) : 128 * (j % 2) + 128]
+            part = part + r * jnp.broadcast_to(rescaled_b[:, j : j + 1], (32, 128))
         for piece in range(4):
             mc_src[sweep, piece] = part[8 * piece : 8 * piece + 8]
         to_plane(
@@ -426,7 +405,7 @@
         gram_got[sweep + 1, col] = gram_src[sweep + 1]
         if sweep == 0:
             lax.fori_loop(TURNS[1], 32, turn, 0, unroll=2)
-            spread(solved_b / scale_a)
+            spread(rescaled_b)
             lax.fori_loop(0, TURNS[2], product_z, 0, unroll=2)
         finish(mc_got.at[sweep], 31, mc_sem.at[sweep, 1])
         mc_mid[sweep] = total(mc_got.at[sweep], 32)
@@ -448,14 +427,23 @@
         if sweep < SWEEPS - 1:
             gram_c = exact(ct, ct, NT)
         else:
-            a_out[...] = solved_a / scale_a
-            b_out[...] = solved_b / scale_b
-            c_out[...] = ct
             at = lax.broadcasted_iota(jnp.int32, (32, 32), 0)
             unit = at == lax.broadcasted_iota(jnp.int32, (32, 32), 1)
-            w_out[...] = jnp.sum(jnp.where(unit, weights, 0.0), axis=0, keepdims=True)
+            across = jnp.sum(jnp.where(unit, weights, 0.0), axis=0, keepdims=True)
+            out[:, 0:256] = solved_a / scale_a
+            out[:, 256:320] = solved_b / scale_b
+            out[:, 320:352] = jnp.broadcast_to(across, (32, 32))
+            out[:, 352:384] = jnp.zeros((32, 32), F32)
+            out[:, 384:512] = ct
     for got, count, sem in sent:
         finish(got, count, sem)
+
+
+def deliver(held, a_out, b_out, c_out, w_out):
+    a_out[...] = held[:, 0:256]
+    b_out[...] = held[:, 256:320]
+    c_out[...] = held[:, 384:512]
+    w_out[...] = held[0:1, 320:352]
 
 
 def shards(total_i, total_j, tensor, factor_b0, factor_c0):
@@ -466,24 +454,16 @@
     def buffer(*shape):
         return pltpu.VMEM(shape, F32)
 
-    results = [
-        jax.ShapeDtypeStruct((32, 256), F32),
-        jax.ShapeDtypeStruct((32, 64), F32),
-        jax.ShapeDtypeStruct((32, 128), F32),
-        jax.ShapeDtypeStruct((1, 32), F32),
-    ]
-    a_t, b_t, c_t, w_t = pl.pallas_call(
+    held = pl.pallas_call(
         functools.partial(kernel, float(total_i), float(total_j)),
-        out_shape=results,
+        out_shape=jax.ShapeDtypeStruct((32, 512), F32),
         in_specs=[pl.BlockSpec(memory_space=pltpu.HBM)] * 3,
-        out_specs=[vmem] * 4,
+        out_specs=vmem,
         scratch_shapes=[
             buffer(32, 64), buffer(32, 128),
             buffer(64, 256, 128),
             pltpu.VMEM((32, 256, 256), BF16),
             pltpu.VMEM((32, 256, 256), BF16),
-            buffer(64, 32, 128),
-            pltpu.VMEM((32, 64, 256), BF16),
             buffer(32, 64, 256),
             buffer(32, 32, 256),
             pltpu.VMEM((16, 2, 256, 256), BF16),
@@ -506,6 +486,17 @@
         pltpu.with_memory_space_constraint(factor_b0.T, pltpu.HBM),
         pltpu.with_memory_space_constraint(factor_c0.T, pltpu.HBM),
     )
+    a_t, b_t, c_t, w_t = pl.pallas_call(
+        deliver,
+        out_shape=[
+            jax.ShapeDtypeStruct((32, 256), F32),
+            jax.ShapeDtypeStruct((32, 64), F32),
+            jax.ShapeDtypeStruct((32, 128), F32),
+            jax.ShapeDtypeStruct((1, 32), F32),
+        ],
+        in_specs=[vmem],
+        out_specs=[vmem] * 4,
+    )(held)
     return a_t.T, b_t.T, c_t.T, w_t[0]
 
 

time: 73.8 us -> 73.3 us (level)
  local copies, waits for them, and re-layouts: 2.34 us -> 0.6 us
  Pallas kernels: 70.7 us -> 71.9 us
    unnamed x4 -> x2, local copies, waits for them, and re-layouts: 2.34 us -> 0.6 us
    pallas_call x0 -> x1, Pallas kernels: none -> 1.47 us  [shards(): pl.pallas_call(deliver, out_shape=[jax.ShapeDtypeStruct((32, 256), F32),...]
where the time goes in v4:
time: 73.3 us; the launch traced here: 73.2 us
  Pallas kernels  71.9 us (98%)
    pallas_call x1, Pallas kernels, shards(): pl.pallas_call(functools.partial(kernel, float(total_i), float(total_j)),...  70.4 us

profile of v4, /device:TPU:1, one launch (start us, length us, event | category | flops | bytes accessed | tf_op | source)
XLA Modules:
  0.0 73.2 jit_solution(929275423770192847)
XLA Ops:
  0.6 70.4 %shard_map.66.held = f32[32,512]{1,0:T(8,128)S(1)} custom-call(f32[256,64,128]{2,1,0:T(8,128)} %tensor.1, f32[32,64]{1,0:T(8,128)} %bitcast.6, f32[32,128]{1,0:T(8,128)} %bitcast.7), custom_call_target="tpu_custom_call" | custom-call | tf_op jit(solution)/shard_map/pallas_call | solution.py:457
  71.1 0.0 copy-start
  71.1 0.6 copy-done
  71.7 1.5 %shard_map.67 = (f32[32,256]{1,0:T(8,128)}, f32[32,64]{1,0:T(8,128)}, f32[32,128]{1,0:T(8,128)}, f32[1,32]{1,0:T(1,128)}) custom-call(f32[32,512]{1,0:T(8,128)} %copy-done), custom_call_target="tpu_custom_call" | custom-call | tf_op jit(solution)/shard_map/pallas_call | solution.py:489
Async XLA Ops:
  71.1 0.6 copy-start

commit v5 on v4

--- a/solution.py
+++ b/solution.py
@@ -55,7 +55,7 @@
     return jnp.broadcast_to(x[at : at + 1, :], (8, 128))
 
 
-def inverse(system):
+def inverse(system, spread_cols, spread_rows):
     row = lax.broadcasted_iota(jnp.int32, (32, 128), 0)
     lane = lax.broadcasted_iota(jnp.int32, (32, 128), 1)
     unit = jnp.where(lane == row + 32, 1.0, 0.0).astype(F32)
@@ -65,8 +65,13 @@
     out = []
     for q in range(4):
         cols = [[lanes(parts[t], 8 * q + c) for t in range(q, 4)] for c in range(8)]
-        rows = [sublanes(parts[q], c) for c in range(8)]
-        small = [[sublanes(cols[b][0], a) if a >= b else None for b in range(8)] for a in range(8)]
+        spread_rows[q] = parts[q]
+        for b in range(8):
+            spread_cols[q, b] = cols[b][0]
+        rows = [jnp.broadcast_to(spread_rows[q, c : c + 1, :], (8, 128)) for c in range(8)]
+        small = [
+            [jnp.broadcast_to(spread_cols[q, b, a : a + 1, :], (8, 128)) if a >= b else None for b in range(8)] for a in range(8)
+        ]
         done = jnp.zeros((8, 128), F32)
         for c in range(8):
             pivot = small[c][c]
@@ -113,7 +118,7 @@
     total_i, total_j,
     tensor, b_in, c_in,
     out,
-    b_here, c_here, staged, high, low, u, y, turned_high, turned_low, chooser, zed,
+    b_here, c_here, staged, high, low, u, y, turned_high, turned_low, chooser, zed, spread_cols, spread_rows,
     gram_src, gram_got, ma_src, ma_got, ma_sum, ma_all,
     mom_src, mom_got, mb_src, mb_got,
     mc_src, mc_got, mc_mid, mc_all,
@@ -141,13 +146,10 @@
     y_offs = [lax.rem(y_at + off, 4) for off in (2, 3, 1, 0)]
 
     def each_col(act):
-        def some(step, carry):
-            base = 4 * lax.rem(z + far_first(step, 8), 8)
+        for z_off in (4, 5, 3, 6, 2, 7, 1):
+            base = 4 * lax.rem(z + z_off, 8)
             for off in y_offs:
                 act(base + off)
-            return carry
-
-        lax.fori_loop(0, 7, some, 0)
         for there in ys[:3]:
             act(there)
 
@@ -335,7 +337,7 @@
         if sweep == 0:
             finish(gram_got.at[0], 31, gram_sem.at[0, 1])
             gram_b = unpack_square(total(gram_got.at[0], 32))
-        inverse_a = inverse(gram_b * gram_c)
+        inverse_a = inverse(gram_b * gram_c, spread_cols, spread_rows)
         finish(ma_got.at[sweep], 31, ma_sem.at[sweep, 1])
         summed = total(ma_got.at[sweep], 32)
         ma_sum[sweep] = summed
@@ -383,7 +385,7 @@
             lax.fori_loop(TURNS[0], TURNS[1], turn, 0, unroll=2)
         finish(mom_got.at[sweep], 7, mom_sem.at[sweep, 1])
         scale_a, gram_a = scales_of(unpack_square(total(mom_got.at[sweep], 8)), total_i)
-        inverse_b = inverse(gram_a * gram_c)
+        inverse_b = inverse(gram_a * gram_c, spread_cols, spread_rows)
         finish(mb_got.at[sweep], 7, mb_sem.at[sweep, 1])
         packed = total(mb_got.at[sweep], 8)
         m_b = jnp.concatenate([packed[:, :64], packed[:, 64:]], axis=0) / scale_a
@@ -416,7 +418,7 @@
             lax.fori_loop(TURNS[2], 16, product_z, 0, unroll=2)
         finish(gram_got.at[sweep + 1], 31, gram_sem.at[sweep + 1, 1])
         scale_b, gram_b = scales_of(unpack_square(total(gram_got.at[sweep + 1], 32)), total_j)
-        inverse_c = inverse(gram_a * gram_b)
+        inverse_c = inverse(gram_a * gram_b, spread_cols, spread_rows)
         finish(mc_all.at[sweep], 31, mcc_sem.at[sweep, 1])
         m_c = jnp.concatenate([total(mc_all.at[sweep, pl.ds(8 * piece, 8)], 8) for piece in range(4)], axis=0) / scale_b
         solved_c = exact(inverse_c, m_c, NN)
@@ -470,6 +472,7 @@
             pltpu.VMEM((16, 2, 256, 256), BF16),
             pltpu.VMEM((2, 512, 256), BF16),
             buffer(16, 256, 256),
+            buffer(4, 8, 8, 128), buffer(4, 8, 128),
             buffer(n + 1, 8, 128), buffer(n + 1, 32, 8, 128),
             buffer(n, 8, 8, 128), buffer(n, 32, 8, 128), buffer(n, 8, 128), buffer(n, 8, 8, 128),
             buffer(n, 8, 128), buffer(n, 8, 8, 128), buffer(n, 16, 128), buffer(n, 8, 16, 128),

time: 73.3 us -> 72.7 us (level)
  no operation moved by 1% of the time
where the time goes in v5:
time: 72.7 us; the launch traced here: 72.5 us
  Pallas kernels  71.3 us (98%)
    pallas_call x1, Pallas kernels, shards(): pl.pallas_call(functools.partial(kernel, float(total_i), float(total_j)),...  69.8 us
    pallas_call x1, Pallas kernels, shards(): pl.pallas_call(deliver, out_shape=[jax.ShapeDtypeStruct((32, 256), F32),...  1.47 us

profile of v5, /device:TPU:1, one launch (start us, length us, event | category | flops | bytes accessed | tf_op | source)
XLA Modules:
  0.0 72.5 jit_solution(369633097759064305)
XLA Ops:
  0.6 69.8 %shard_map.66.held = f32[32,512]{1,0:T(8,128)S(1)} custom-call(f32[256,64,128]{2,1,0:T(8,128)} %tensor.1, f32[32,64]{1,0:T(8,128)} %bitcast.6, f32[32,128]{1,0:T(8,128)} %bitcast.7), custom_call_target="tpu_custom_call" | custom-call | tf_op jit(solution)/shard_map/pallas_call | solution.py:459
  70.5 0.0 copy-start
  70.5 0.6 copy-done
  71.1 1.5 %shard_map.67 = (f32[32,256]{1,0:T(8,128)}, f32[32,64]{1,0:T(8,128)}, f32[32,128]{1,0:T(8,128)}, f32[1,32]{1,0:T(1,128)}) custom-call(f32[32,512]{1,0:T(8,128)} %copy-done), custom_call_target="tpu_custom_call" | custom-call | tf_op jit(solution)/shard_map/pallas_call | solution.py:492
Async XLA Ops:
  70.5 0.6 copy-start
